TPU v7x, 1024 devices: a whole 4x8x16 slice. The times are simulated.
1024 devices in a mesh: wide: 32 (over x_hi, y, core), narrow: 32 (over x_lo, z).
Axes of the slice: x: 4 (x_hi: 2, x_lo: 2; x = x_hi * 2 + x_lo), y: 8, z: 16, core: 2. Of those that a mesh axis runs over, the one named last changes fastest.
Arguments:
- points: bfloat16 [262144, 1024], P(('wide', 'narrow')), may hold values from -6 to 6
- centers: bfloat16 [3, 4096, 1024], P(None, 'wide'), may hold values from -6 to 6
- moving: int32 [3, 2048], P(None, ('wide', 'narrow')), may hold values from 0 to 1, as said below
- sent_counts: int32 [3, 1024], P(None, ('wide', 'narrow')), may hold values from 1 to 2, as said below
Outputs:
- new_centers: float32 [3, 4096, 1024], P(None, 'wide')
Inputs may be any that keep to these rules, and one draw needn't show every extreme that they name: `moving`: in section s a device's number of entries 1 equals its entry of sent_counts and its partner's count (partner: wide index differing in bit s, same narrow index). `sent_counts`: A device's count equals its partner's in that section; in every section some pair of partners sends exactly 2 blocks each.
All inputs are finite; a program needn't handle non-finite values.
Results may differ from a plain program's by a relative error of at most 0.0055.
Values may be sent and summed in bfloat16 or wider, within the bound.
No kernel may reach another device: no remote copies, remote signals or barrier semaphores. Data moves between devices by JAX's collectives and lax.ppermute only.
A program may use at most 32 MiB of HBM per device.

v0:
```python
import jax
import jax.numpy as jnp
from jax import lax
from jax.sharding import PartitionSpec as P

CAP = 2


EPS = 1e-06
SHARPNESS = 80.0


def partner(value, axis, stride):
    mask = 2**stride
    pairs = [(source, source ^ mask) for source in range(lax.axis_size(axis))]
    return lax.ppermute(value, axis, pairs)


def unit_rows(values):
    widened = values.astype(jnp.float32)
    return widened * lax.rsqrt(jnp.mean(widened * widened, axis=-1, keepdims=True) + EPS)


def local_sums(rows, section_centers):
    width = rows.shape[1]
    unit = unit_rows(rows).astype(jnp.bfloat16)
    cunit = unit_rows(section_centers).astype(jnp.bfloat16)
    scores = lax.dot_general(
        unit, cunit, (((1,), (1,)), ((), ())), preferred_element_type=jnp.float32
    ) * (SHARPNESS / width)
    raised = jnp.exp(scores)
    weights = (raised / jnp.sum(raised, axis=-1, keepdims=True)).astype(jnp.bfloat16)
    return lax.dot_general(
        weights, unit, (((0,), (0,)), ((), ())), preferred_element_type=jnp.float32
    )


def reduce_centroids(stacked):
    summed = lax.psum(stacked, "narrow")
    return unit_rows(summed)


def on_device(points, centers, moving, sent_counts):
    rows_dev, width = points.shape
    sections, blocks = moving.shape
    layout = points.reshape(blocks, rows_dev // blocks * width)
    slot_ids = jnp.arange(CAP, dtype=jnp.int32)
    block_ids = jnp.arange(blocks, dtype=jnp.int32)
    updated = []
    for section_num in range(sections):
        flags = moving[section_num]
        ranks = jnp.cumsum(flags) - 1
        chosen = (flags == 1) & (ranks < sent_counts[section_num, 0])
        match = chosen[None, :] & (ranks[None, :] == slot_ids[:, None])
        source = jnp.sum(jnp.where(match, block_ids[None, :], 0), axis=1)
        valid = jnp.any(match, axis=1)
        outgoing = jnp.where(valid[:, None], layout[source], jnp.zeros((), jnp.bfloat16))
        incoming = partner(outgoing, "wide", section_num)
        placed = incoming[jnp.clip(ranks, 0, CAP - 1)]
        layout = jnp.where(chosen[:, None], placed, layout)
        total = local_sums(layout.reshape(rows_dev, width), centers[section_num])
        updated.append(reduce_centroids(total[None])[0])
    return jnp.stack(updated)


def solution(mesh):
    return jax.shard_map(
        on_device,
        mesh=mesh,
        in_specs=(
            P(("wide", "narrow"), None),
            P(None, "wide", None),
            P(None, ("wide", "narrow")),
            P(None, ("wide", "narrow")),
        ),
        out_specs=P(None, "wide", None),
        check_vma=False,
    )
```

profile of v0, /device:TPU:16, one launch (start us, length us, event | category | flops | bytes accessed | tf_op | source)
XLA Modules:
  0.0 370.6 jit_solution(16806840120433794484)
XLA Ops:
  6.5 1.4 fusion.58
  8.0 0.9 fusion.57
  8.9 0.2 reduce-window.10
  9.1 0.7 fusion.38
  9.8 0.1 fusion.41
  10.0 1.4 reshape.315
  11.5 0.4 fusion.56
  11.8 0.9 gather_fusion
  12.7 0.9 gather_fusion.1
  13.6 0.6 broadcast_select_fusion.4
  14.2 1.9 collective-permute-start
  16.3 0.2 reduce-window.14
  16.4 0.7 fusion.36
  17.1 0.7 bitcast_and_fusion.1
  17.9 0.2 reduce-window.11
  18.1 0.6 fusion.37
  18.7 0.6 bitcast_and_fusion.3
  19.3 0.7 bitcast_and_fusion.5
  19.9 0.1 fusion.40
  20.4 0.2 fusion.9
  21.0 0.4 fusion.55
  21.3 0.9 gather_fusion.3
  22.2 0.9 gather_fusion.2
  23.1 0.2 constant_dynamic-update-slice_fusion.1
  23.3 0.2 constant_dynamic-update-slice_fusion
  23.5 0.6 broadcast_select_fusion.1
  24.2 0.5 gather.26
  24.6 0.4 fusion.54
  25.0 0.9 gather_fusion.4
  25.9 0.9 gather_fusion.5
  26.8 0.6 broadcast_select_fusion.3
  27.4 3.7 collective-permute-start.1
  31.1 0.4 fusion.3
  31.5 0.4 fusion.61
  31.9 1.1 convolution_bitcast_fusion.2
  33.0 10.6 %collective-permute-done.1 = bf16[2,131072]{1,0:T(2,128)(2,1)S(1)} collective-permute-done((bf16[2,131072]{1,0:T(2,128)(2,1)S(1)}, bf16[2,131072]{1,0:T(2,128)(2,1)S(1)}, u32[]{:S(2)}, u32[]{:S(2)}) %collective-permute-start.1) | collective-permute-done | bytes 524320 | tf_op jit(solution)/shard_map/ppermute | solution.py:16
  43.6 0.4 fusion.53
  44.0 0.9 gather_fusion.7
  44.9 0.9 gather_fusion.6
  45.8 0.2 constant_dynamic-update-slice_fusion.3
  46.0 0.2 constant_dynamic-update-slice_fusion.2
  46.2 0.6 broadcast_select_fusion
  46.8 0.5 gather.29
  47.3 0.4 fusion.52
  47.7 0.9 gather_fusion.8
  48.6 0.9 gather_fusion.9
  49.4 0.6 broadcast_select_fusion.2
  50.1 14.9 %collective-permute-start.2 = (bf16[2,131072]{1,0:T(2,128)(2,1)S(1)}, bf16[2,131072]{1,0:T(2,128)(2,1)S(1)}, u32[]{:S(2)}, u32[]{:S(2)}) collective-permute-start(bf16[2,131072]{1,0:T(2,128)(2,1)S(1)} %broadcast_select_fusion.2), channel_id=1, source_target_pairs={{0,128},{32,160},{64,192},{96,224},{128,0},{160,32},{192,64},{224,... | collective-permute-start | bytes 1572872 | tf_op jit(solution)/shard_map/ppermute | solution.py:16
  65.0 0.4 fusion.5
  65.3 0.4 fusion.60
  65.7 1.1 convolution_bitcast_fusion.1
  66.9 20.3 %collective-permute-done.2 = bf16[2,131072]{1,0:T(2,128)(2,1)S(1)} collective-permute-done((bf16[2,131072]{1,0:T(2,128)(2,1)S(1)}, bf16[2,131072]{1,0:T(2,128)(2,1)S(1)}, u32[]{:S(2)}, u32[]{:S(2)}) %collective-permute-start.2) | collective-permute-done | bytes 524320 | tf_op jit(solution)/shard_map/ppermute | solution.py:16
  87.2 0.4 fusion.51
  87.5 0.9 gather_fusion.10
  88.4 0.9 gather_fusion.11
  89.3 0.5 pad_maximum_fusion.1
  89.8 0.5 gather.32
  90.2 0.4 fusion.7
  90.6 0.4 fusion.59
  91.0 1.1 convolution_bitcast_fusion
  92.2 267.4 %all-reduce.3.cloned.1.call-done = (f32[1,128,1024]{2,1,0:T(8,128)}, f32[1,128,1024]{2,1,0:T(8,128)}, f32[1,128,1024]{2,1,0:T(8,128)}) async-done(((f32[1,128,1024]{2,1,0:T(8,128)}, f32[1,128,1024]{2,1,0:T(8,128)}, f32[1,128,1024]{2,1,0:T(8,128)}), (f32[1,128,1024]{2,1,0:T(8,128)}, f32[1,128,1024]{2,1,0:T(8,128)}, f32[1,128,1024]{2,1,0:T(8,128)})) %all-reduce.3.cloned.1.call-update) | async-done | bytes 1572880 | tf_op jit(solution)/shard_map/psum | solution.py:39
  359.5 1.2 multiply_reduce_fusion
  360.8 1.1 broadcast_multiply_fusion
  362.5 1.2 pad_maximum_fusion
  (44 shorter events, 1.6 us)
Async XLA Ops:
  6.5 353.0 %all-reduce.3.cloned.1.call-start = ((), (), s32[]{:S(2)}) async-start(), calls=%async_computation | async-start | bytes 3145728 | tf_op jit(solution)/shard_map/psum | solution.py:39
  12.7 7.7 %copy-start.3 = (bf16[3,128,1024]{2,1,0:T(8,128)(2,1)S(1)}, bf16[3,128,1024]{2,1,0:T(8,128)(2,1)}, u32[]{:S(2)}) copy-start(bf16[3,128,1024]{2,1,0:T(8,128)(2,1)} %param.5) | copy-start | bytes 2359300
  14.2 6.7 %collective-permute-start = (bf16[2,131072]{1,0:T(2,128)(2,1)S(1)}, bf16[2,131072]{1,0:T(2,128)(2,1)S(1)}, u32[]{:S(2)}, u32[]{:S(2)}) collective-permute-start(bf16[2,131072]{1,0:T(2,128)(2,1)S(1)} %broadcast_select_fusion.4), channel_id=1, source_target_pairs={{0,32},{32,0},{64,96},{96,64},{128,160},{160,128},{192,224},{224,1... | collective-permute-start | bytes 1572872 | tf_op jit(solution)/shard_map/ppermute | solution.py:16
  25.9 5.2 %copy-start = (bf16[256,1024]{1,0:T(8,128)(2,1)S(1)}, bf16[256,1024]{1,0:T(8,128)(2,1)}, u32[]{:S(2)}) copy-start(bf16[256,1024]{1,0:T(8,128)(2,1)} %param.4) | copy-start | bytes 1572868
  27.4 16.2 %collective-permute-start.1 = (bf16[2,131072]{1,0:T(2,128)(2,1)S(1)}, bf16[2,131072]{1,0:T(2,128)(2,1)S(1)}, u32[]{:S(2)}, u32[]{:S(2)}) collective-permute-start(bf16[2,131072]{1,0:T(2,128)(2,1)S(1)} %broadcast_select_fusion.3), channel_id=1, source_target_pairs={{0,64},{32,96},{64,0},{96,32},{128,192},{160,224},{192,128},{224,1... | collective-permute-start | bytes 1572872 | tf_op jit(solution)/shard_map/ppermute | solution.py:16
  50.1 37.1 %collective-permute-start.2 = (bf16[2,131072]{1,0:T(2,128)(2,1)S(1)}, bf16[2,131072]{1,0:T(2,128)(2,1)S(1)}, u32[]{:S(2)}, u32[]{:S(2)}) collective-permute-start(bf16[2,131072]{1,0:T(2,128)(2,1)S(1)} %broadcast_select_fusion.2), channel_id=1, source_target_pairs={{0,128},{32,160},{64,192},{96,224},{128,0},{160,32},{192,64},{224,... | collective-permute-start | bytes 1572872 | tf_op jit(solution)/shard_map/ppermute | solution.py:16
  359.5 2.4 copy-start.2
  359.5 2.7 copy-start.1
Sparse Core Ops, SparseCore 0:
  92.3 267.1 all-reduce.2
where the time goes:
time: 371 us
  waiting for transfers between devices  298 us (80%)
  starting transfers between devices  20.5 us (6%)
  local copies, waits for them, and re-layouts  19.2 us (5%)
  other arithmetic  14.1 us (4%)
  between operations  13.8 us (4%)
  matrix products  4.65 us (1%)
    psum x1, waiting for transfers between devices, reduce_centroids(): summed = lax.psum(stacked, 'narrow')  267 us
    ppermute x3, waiting for transfers between devices, partner(): return lax.ppermute(value, axis, pairs)  30.9 us
    ppermute x3, starting transfers between devices, partner(): return lax.ppermute(value, axis, pairs)  20.5 us
    gather x12, local copies, waits for them, and re-layouts, on_device(): placed = incoming[jnp.clip(ranks, 0, CAP - 1)]  7.81 us
  transfers between devices with their start and end apart: 4, of which 3 were waited for; matrix products, arithmetic and copies ran while one was open for 2% of the time, Pallas kernels for 0%

commit v1 on v0

v1 whole, which is shorter than its diff:
```python
import jax
import jax.numpy as jnp
from jax import lax
from jax.sharding import PartitionSpec as P

EPS = 1e-06
SHARPNESS = 80.0
LANES = 128


def partner(value, axis, mask):
    pairs = [(source, source ^ mask) for source in range(lax.axis_size(axis))]
    return lax.ppermute(value, axis, pairs)


def unit_rows(values):
    widened = values.astype(jnp.float32)
    return widened * lax.rsqrt(jnp.mean(widened * widened, axis=-1, keepdims=True) + EPS)


def local_sums(unit, cunit):
    width = unit.shape[1]
    scores = lax.dot_general(
        unit, cunit, (((1,), (1,)), ((), ())), preferred_element_type=jnp.float32
    ) * (SHARPNESS / width)
    raised = jnp.exp(scores)
    weights = (raised / jnp.sum(raised, axis=-1, keepdims=True)).astype(jnp.bfloat16)
    return lax.dot_general(
        weights, unit, (((0,), (0,)), ((), ())), preferred_element_type=jnp.float32
    )


def rings():
    number = lax.axis_size("narrow")
    return [list(range(number // 2)), list(range(number // 2, number))]


def exchange(values):
    return lax.all_to_all(values, "narrow", 0, 0, axis_index_groups=rings(), tiled=True)


def side():
    return lax.axis_index("narrow") // (lax.axis_size("narrow") // 2)


def pair_sums(total):
    half = total.shape[0] // 2
    mine = side()
    kept = lax.dynamic_slice_in_dim(total, mine * half, half)
    sent = lax.dynamic_slice_in_dim(total, (1 - mine) * half, half).astype(jnp.bfloat16)
    taken = partner(sent, "narrow", lax.axis_size("narrow") // 2)
    return kept + taken.astype(jnp.float32)


def to_chunks(rows):
    return rows.reshape(lax.axis_size("narrow") // 2, -1, LANES)


def to_all(chunk):
    return jnp.broadcast_to(chunk[None], (lax.axis_size("narrow") // 2,) + chunk.shape)


def join_pair(mine):
    other = partner(mine, "narrow", lax.axis_size("narrow") // 2)
    is_upper = side() == 1
    lower = jnp.where(is_upper, other, mine)
    upper = jnp.where(is_upper, mine, other)
    return jnp.concatenate([lower, upper], axis=1).astype(jnp.float32)


def norm_chunk(chunk, width):
    rows = chunk.reshape(-1, width // LANES, LANES)
    mean = jnp.mean(rows * rows, axis=(1, 2), keepdims=True)
    return (rows * lax.rsqrt(mean + EPS)).reshape(chunk.shape).astype(jnp.bfloat16)


def chosen_slots(moving, sent_counts):
    flags, counts = moving.T, sent_counts.T
    ranks = jnp.concatenate([flags[:1], flags[:1] + flags[1:]]) - 1
    chosen = ((flags == 1) & (ranks < counts)).astype(jnp.int32)
    chosen = lax.optimization_barrier(chosen)
    return [[chosen[slot, section] == 1 for slot in range(2)] for section in range(chosen.shape[1])]


def on_device(points, centers, moving, sent_counts):
    rows_dev, width = points.shape
    sections, _ = moving.shape
    half = rows_dev // 2
    end = sections - 1
    chosen = chosen_slots(moving, sent_counts)
    unit = unit_rows(points).astype(jnp.bfloat16)
    cunit = unit_rows(centers).astype(jnp.bfloat16)
    far = partner(cunit[end], "wide", 2**end)
    first, second = unit[:half], unit[half:]
    parts = []
    for section in range(end):
        at_first, at_second = chosen[section]
        outgoing = jnp.concatenate([jnp.where(at_first, first, second), second])
        incoming = partner(outgoing, "wide", 2**section)
        lower, upper = incoming[:half], incoming[half:]
        first = jnp.where(at_first, lower, first)
        second = jnp.where(at_second, jnp.where(at_first, upper, lower), second)
        total = local_sums(jnp.concatenate([first, second]), cunit[section])
        parts.append(to_chunks(pair_sums(total).astype(jnp.bfloat16)))
    leaving = chosen[end]
    sums = [
        local_sums(block, jnp.where(leaves, far, cunit[end]))
        for block, leaves in zip((first, second), leaving)
    ]
    stays = sum(jnp.where(leaves, 0.0, part) for leaves, part in zip(leaving, sums))
    leaves = sum(jnp.where(leaves, part, 0.0) for leaves, part in zip(leaving, sums))
    both = jnp.concatenate([stays.reshape(2, half // 2, width), leaves.reshape(2, half // 2, width)], axis=1)
    paired = pair_sums(both.reshape(2 * half, width))
    gone = partner(paired[half // 2 :].astype(jnp.bfloat16), "wide", 2**end)
    paired = paired[: half // 2] + gone.astype(jnp.float32)
    parts.append(to_chunks(paired.astype(jnp.bfloat16)))
    taken = exchange(jnp.concatenate(parts, axis=1))
    summed = jnp.sum(taken.astype(jnp.float32), axis=0)
    chunk = norm_chunk(summed, width)
    taken = exchange(to_all(chunk))
    taken = jnp.moveaxis(taken.reshape(taken.shape[0], sections, -1, LANES), 1, 0)
    return join_pair(taken.reshape(sections, half // 2, width))


def solution(mesh):
    return jax.shard_map(
        on_device,
        mesh=mesh,
        in_specs=(
            P(("wide", "narrow"), None),
            P(None, "wide", None),
            P(None, ("wide", "narrow")),
            P(None, ("wide", "narrow")),
        ),
        out_specs=P(None, "wide", None),
        check_vma=False,
    )
```

time: 371 us -> 138 us (0.37)
  the two profiles are of different devices: /device:TPU:16 before, /device:TPU:26 now
where the time goes in v1:
time: 138 us; the launch traced here: 137 us
  blocking collectives  60.7 us (44%)
  starting transfers between devices  31.3 us (23%)
  waiting for transfers between devices  29.8 us (22%)
  other arithmetic  6.66 us (5%)
  between operations  4.19 us (3%)
  matrix products  3.04 us (2%)
  local copies, waits for them, and re-layouts  1.48 us (1%)
    all_to_all x2, blocking collectives, exchange(): lax.all_to_all(values, 'narrow', 0, 0, axis_index_groups=rings(), tiled=T...  60.7 us
    ppermute x8, starting transfers between devices, partner(): return lax.ppermute(value, axis, pairs)  31.3 us
    ppermute x8, waiting for transfers between devices, partner(): return lax.ppermute(value, axis, pairs)  29.8 us
  transfers between devices with their start and end apart: 8, of which 6 were waited for; matrix products, arithmetic and copies ran while one was open for 1% of the time, Pallas kernels for 0%

profile of v1, /device:TPU:26, one launch (start us, length us, event | category | flops | bytes accessed | tf_op | source)
XLA Modules:
  0.0 137.1 jit_solution(3547436097551703515)
XLA Ops:
  0.0 0.8 fusion.29
  0.8 0.7 and_convert_fusion
  1.5 0.7 fusion.28
  2.1 1.2 fusion.6
  3.4 0.0 copy-start
  3.4 1.3 fusion.7
  5.4 1.9 %collective-permute-start = (bf16[256,1024]{1,0:T(8,128)(2,1)S(1)}, bf16[256,1024]{1,0:T(8,128)(2,1)S(1)}, u32[]{:S(2)}, u32[]{:S(2)}) collective-permute-start(bf16[256,1024]{1,0:T(8,128)(2,1)S(1)} %pad_maximum_fusion.3), channel_id=1, source_target_pairs={{0,32},{32,0},{64,96},{96,64},{128,160},{160,128},{192,224},{224,1... | collective-permute-start | bytes 1572872 | tf_op jit(solution)/shard_map/ppermute | solution.py:13
  7.3 0.0 copy-done
  7.3 0.2 fusion
  8.9 0.2 fusion.1
  9.1 0.1 collective-permute-done
  9.2 0.1 broadcast_select_fusion.3
  9.3 2.4 %collective-permute-start.2 = (bf16[256,1024]{1,0:T(8,128)(2,1)S(1)}, bf16[256,1024]{1,0:T(8,128)(2,1)S(1)}, u32[]{:S(2)}, u32[]{:S(2)}) collective-permute-start(bf16[256,1024]{1,0:T(8,128)(2,1)S(1)} %pad_maximum_fusion.1), channel_id=1, source_target_pairs={{0,64},{32,96},{64,0},{96,32},{128,192},{160,224},{192,128},{224,1... | collective-permute-start | bytes 1572872 | tf_op jit(solution)/shard_map/ppermute | solution.py:13
  11.7 0.3 fusion.33
  12.0 0.2 fusion.9
  12.3 2.4 %collective-permute-start.1 = (bf16[64,1024]{1,0:T(8,128)(2,1)S(1)}, bf16[64,1024]{1,0:T(8,128)(2,1)S(1)}, u32[]{:S(2)}, u32[]{:S(2)}) collective-permute-start(bf16[64,1024]{1,0:T(8,128)(2,1)S(1)} %dynamic-slice_convert_fusion.2), channel_id=1, source_target_pairs={{0,16},{1,17},{2,18},{3,19},{4,20},{5,21},{6,22},{7,23},{8,24},{9,... | collective-permute-start | bytes 393224 | tf_op jit(solution)/shard_map/ppermute | solution.py:13
  14.8 14.9 %collective-permute-start.4 = (bf16[128,1024]{1,0:T(8,128)(2,1)S(1)}, bf16[128,1024]{1,0:T(8,128)(2,1)}, u32[]{:S(2)}, u32[]{:S(2)}) collective-permute-start(bf16[128,1024]{1,0:T(8,128)(2,1)S(1)} %slice_bitcast_fusion), channel_id=1, source_target_pairs={{0,128},{32,160},{64,192},{96,224},{128,0},{160,32},{192,64},{224,... | collective-permute-start | bytes 786440 | tf_op jit(solution)/shard_map/ppermute | solution.py:13
  31.6 0.0 collective-permute-done.1
  31.7 0.1 reshape.86
  31.7 0.0 collective-permute-done.2
  31.7 0.1 broadcast_select_fusion.2
  31.8 0.3 fusion.32
  32.1 9.3 %collective-permute-done.4 = bf16[128,1024]{1,0:T(8,128)(2,1)} collective-permute-done((bf16[128,1024]{1,0:T(8,128)(2,1)S(1)}, bf16[128,1024]{1,0:T(8,128)(2,1)}, u32[]{:S(2)}, u32[]{:S(2)}) %collective-permute-start.4) | collective-permute-done | bytes 262176 | tf_op jit(solution)/shard_map/ppermute | solution.py:13
  41.4 1.2 fusion.31
  42.6 0.2 fusion.19
  42.8 0.3 fusion.30
  43.1 0.2 select_add_fusion.1
  43.3 0.1 pad_maximum_fusion
  43.5 1.9 %collective-permute-start.5 = (bf16[128,1024]{1,0:T(8,128)(2,1)S(1)}, bf16[128,1024]{1,0:T(8,128)(2,1)S(1)}, u32[]{:S(2)}, u32[]{:S(2)}) collective-permute-start(bf16[128,1024]{1,0:T(8,128)(2,1)S(1)} %dynamic-slice_convert_fusion), channel_id=1, source_target_pairs={{0,16},{1,17},{2,18},{3,19},{4,20},{5,21},{6,22},{7,23},{8,24},{9,... | collective-permute-start | bytes 786440 | tf_op jit(solution)/shard_map/ppermute | solution.py:13
  45.4 0.2 fusion.8
  45.7 3.9 %collective-permute-start.3 = (bf16[64,1024]{1,0:T(8,128)(2,1)S(1)}, bf16[64,1024]{1,0:T(8,128)(2,1)S(1)}, u32[]{:S(2)}, u32[]{:S(2)}) collective-permute-start(bf16[64,1024]{1,0:T(8,128)(2,1)S(1)} %dynamic-slice_convert_fusion.1), channel_id=1, source_target_pairs={{0,16},{1,17},{2,18},{3,19},{4,20},{5,21},{6,22},{7,23},{8,24},{9,... | collective-permute-start | bytes 393224 | tf_op jit(solution)/shard_map/ppermute | solution.py:13
  49.6 4.9 %collective-permute-done.5 = bf16[128,1024]{1,0:T(8,128)(2,1)S(1)} collective-permute-done((bf16[128,1024]{1,0:T(8,128)(2,1)S(1)}, bf16[128,1024]{1,0:T(8,128)(2,1)S(1)}, u32[]{:S(2)}, u32[]{:S(2)}) %collective-permute-start.5) | collective-permute-done | bytes 262176 | tf_op jit(solution)/shard_map/ppermute | solution.py:13
  54.5 0.1 convert_add_fusion
  54.6 1.9 %collective-permute-start.6 = (bf16[64,1024]{1,0:T(8,128)(2,1)S(1)}, bf16[64,1024]{1,0:T(8,128)(2,1)S(1)}, u32[]{:S(2)}, u32[]{:S(2)}) collective-permute-start(bf16[64,1024]{1,0:T(8,128)(2,1)S(1)} %slice.122), channel_id=1, source_target_pairs={{0,128},{32,160},{64,192},{96,224},{128,0},{160,32},{192,64},{224,... | collective-permute-start | bytes 393224 | tf_op jit(solution)/shard_map/ppermute | solution.py:13
  56.6 0.8 collective-permute-done.3
  57.4 0.1 reshape.87
  57.4 6.9 %collective-permute-done.6 = bf16[64,1024]{1,0:T(8,128)(2,1)S(1)} collective-permute-done((bf16[64,1024]{1,0:T(8,128)(2,1)S(1)}, bf16[64,1024]{1,0:T(8,128)(2,1)S(1)}, u32[]{:S(2)}, u32[]{:S(2)}) %collective-permute-start.6) | collective-permute-done | bytes 131104 | tf_op jit(solution)/shard_map/ppermute | solution.py:13
  64.4 0.1 reshape.91
  64.5 31.1 %all_to_all.10 = bf16[16,96,128]{2,1,0:T(8,128)(2,1)S(1)} all-to-all(bf16[16,96,128]{2,1,0:T(8,128)(2,1)S(1)} %pad_maximum_fusion.5), channel_id=1, replica_groups={{0,1,2,3,4,5,6,7,8,9,10,11,12,13,14,15},{16,17,18,19,20,21,22,23,24,25,..., dimensions={0} | all-to-all | bytes 786432 | tf_op jit(solution)/shard_map/all_to_all | solution.py:39
  95.6 0.1 convert_reduce_fusion
  95.6 0.1 multiply_reduce_fusion
  95.7 0.1 reduce_sum.87
  95.8 0.1 reduce_sum.88
  96.0 0.1 mul.84
  96.0 0.1 mul.85
  96.1 0.1 multiply_convert_fusion
  96.2 0.1 broadcast_in_dim.11
  96.3 29.6 %all_to_all.11 = bf16[16,96,128]{2,1,0:T(8,128)(2,1)S(1)} all-to-all(bf16[16,96,128]{2,1,0:T(8,128)(2,1)S(1)} %broadcast_in_dim.11), channel_id=1, replica_groups={{0,1,2,3,4,5,6,7,8,9,10,11,12,13,14,15},{16,17,18,19,20,21,22,23,24,25,..., dimensions={0} | all-to-all | bytes 786432 | tf_op jit(solution)/shard_map/all_to_all | solution.py:39
  125.9 0.2 reshape.93
  126.1 1.9 %collective-permute-start.7 = (bf16[3,64,1024]{2,1,0:T(8,128)(2,1)S(1)}, bf16[3,64,1024]{2,1,0:T(8,128)(2,1)S(1)}, u32[]{:S(2)}, u32[]{:S(2)}) collective-permute-start(bf16[3,64,1024]{2,1,0:T(8,128)(2,1)S(1)} %reshape.93), channel_id=1, source_target_pairs={{0,16},{1,17},{2,18},{3,19},{4,20},{5,21},{6,22},{7,23},{8,24},{9,... | collective-permute-start | bytes 1179656 | tf_op jit(solution)/shard_map/ppermute | solution.py:13
  128.0 7.7 %collective-permute-done.7 = bf16[3,64,1024]{2,1,0:T(8,128)(2,1)S(1)} collective-permute-done((bf16[3,64,1024]{2,1,0:T(8,128)(2,1)S(1)}, bf16[3,64,1024]{2,1,0:T(8,128)(2,1)S(1)}, u32[]{:S(2)}, u32[]{:S(2)}) %collective-permute-start.7) | collective-permute-done | bytes 393248 | tf_op jit(solution)/shard_map/ppermute | solution.py:13
  135.7 0.1 broadcast_select_fusion.1
  135.8 1.3 maximum_convert_fusion
  (16 shorter events, 0.4 us)
Async XLA Ops:
  3.4 3.9 %copy-start = (bf16[3,128,1024]{2,1,0:T(8,128)(2,1)S(1)}, bf16[3,128,1024]{2,1,0:T(8,128)(2,1)}, u32[]{:S(2)}) copy-start(bf16[3,128,1024]{2,1,0:T(8,128)(2,1)} %param.5) | copy-start | bytes 2359300
  5.4 3.8 %collective-permute-start = (bf16[256,1024]{1,0:T(8,128)(2,1)S(1)}, bf16[256,1024]{1,0:T(8,128)(2,1)S(1)}, u32[]{:S(2)}, u32[]{:S(2)}) collective-permute-start(bf16[256,1024]{1,0:T(8,128)(2,1)S(1)} %pad_maximum_fusion.3), channel_id=1, source_target_pairs={{0,32},{32,0},{64,96},{96,64},{128,160},{160,128},{192,224},{224,1... | collective-permute-start | bytes 1572872 | tf_op jit(solution)/shard_map/ppermute | solution.py:13
  9.3 22.4 %collective-permute-start.2 = (bf16[256,1024]{1,0:T(8,128)(2,1)S(1)}, bf16[256,1024]{1,0:T(8,128)(2,1)S(1)}, u32[]{:S(2)}, u32[]{:S(2)}) collective-permute-start(bf16[256,1024]{1,0:T(8,128)(2,1)S(1)} %pad_maximum_fusion.1), channel_id=1, source_target_pairs={{0,64},{32,96},{64,0},{96,32},{128,192},{160,224},{192,128},{224,1... | collective-permute-start | bytes 1572872 | tf_op jit(solution)/shard_map/ppermute | solution.py:13
  12.3 19.3 %collective-permute-start.1 = (bf16[64,1024]{1,0:T(8,128)(2,1)S(1)}, bf16[64,1024]{1,0:T(8,128)(2,1)S(1)}, u32[]{:S(2)}, u32[]{:S(2)}) collective-permute-start(bf16[64,1024]{1,0:T(8,128)(2,1)S(1)} %dynamic-slice_convert_fusion.2), channel_id=1, source_target_pairs={{0,16},{1,17},{2,18},{3,19},{4,20},{5,21},{6,22},{7,23},{8,24},{9,... | collective-permute-start | bytes 393224 | tf_op jit(solution)/shard_map/ppermute | solution.py:13
  14.8 26.6 %collective-permute-start.4 = (bf16[128,1024]{1,0:T(8,128)(2,1)S(1)}, bf16[128,1024]{1,0:T(8,128)(2,1)}, u32[]{:S(2)}, u32[]{:S(2)}) collective-permute-start(bf16[128,1024]{1,0:T(8,128)(2,1)S(1)} %slice_bitcast_fusion), channel_id=1, source_target_pairs={{0,128},{32,160},{64,192},{96,224},{128,0},{160,32},{192,64},{224,... | collective-permute-start | bytes 786440 | tf_op jit(solution)/shard_map/ppermute | solution.py:13
  43.5 11.1 %collective-permute-start.5 = (bf16[128,1024]{1,0:T(8,128)(2,1)S(1)}, bf16[128,1024]{1,0:T(8,128)(2,1)S(1)}, u32[]{:S(2)}, u32[]{:S(2)}) collective-permute-start(bf16[128,1024]{1,0:T(8,128)(2,1)S(1)} %dynamic-slice_convert_fusion), channel_id=1, source_target_pairs={{0,16},{1,17},{2,18},{3,19},{4,20},{5,21},{6,22},{7,23},{8,24},{9,... | collective-permute-start | bytes 786440 | tf_op jit(solution)/shard_map/ppermute | solution.py:13
  45.7 11.7 %collective-permute-start.3 = (bf16[64,1024]{1,0:T(8,128)(2,1)S(1)}, bf16[64,1024]{1,0:T(8,128)(2,1)S(1)}, u32[]{:S(2)}, u32[]{:S(2)}) collective-permute-start(bf16[64,1024]{1,0:T(8,128)(2,1)S(1)} %dynamic-slice_convert_fusion.1), channel_id=1, source_target_pairs={{0,16},{1,17},{2,18},{3,19},{4,20},{5,21},{6,22},{7,23},{8,24},{9,... | collective-permute-start | bytes 393224 | tf_op jit(solution)/shard_map/ppermute | solution.py:13
  54.6 9.7 %collective-permute-start.6 = (bf16[64,1024]{1,0:T(8,128)(2,1)S(1)}, bf16[64,1024]{1,0:T(8,128)(2,1)S(1)}, u32[]{:S(2)}, u32[]{:S(2)}) collective-permute-start(bf16[64,1024]{1,0:T(8,128)(2,1)S(1)} %slice.122), channel_id=1, source_target_pairs={{0,128},{32,160},{64,192},{96,224},{128,0},{160,32},{192,64},{224,... | collective-permute-start | bytes 393224 | tf_op jit(solution)/shard_map/ppermute | solution.py:13
  126.1 9.7 %collective-permute-start.7 = (bf16[3,64,1024]{2,1,0:T(8,128)(2,1)S(1)}, bf16[3,64,1024]{2,1,0:T(8,128)(2,1)S(1)}, u32[]{:S(2)}, u32[]{:S(2)}) collective-permute-start(bf16[3,64,1024]{2,1,0:T(8,128)(2,1)S(1)} %reshape.93), channel_id=1, source_target_pairs={{0,16},{1,17},{2,18},{3,19},{4,20},{5,21},{6,22},{7,23},{8,24},{9,... | collective-permute-start | bytes 1179656 | tf_op jit(solution)/shard_map/ppermute | solution.py:13

commit v2 on v1

--- a/solution.py
+++ b/solution.py
@@ -32,40 +32,38 @@
 
 def rings():
     number = lax.axis_size("narrow")
-    return [list(range(number // 2)), list(range(number // 2, number))]
+    ring = number // 2
+    return [list(range(base + odd, base + ring, 2)) for base in (0, ring) for odd in (0, 1)]
 
 
-def exchange(values):
-    return lax.all_to_all(values, "narrow", 0, 0, axis_index_groups=rings(), tiled=True)
+def squares():
+    number = lax.axis_size("narrow")
+    ring = number // 2
+    return [[at, at + 1, at + ring, at + ring + 1] for at in range(0, ring, 2)]
+
+
+def exchange(values, groups):
+    return lax.all_to_all(values, "narrow", 0, 0, axis_index_groups=groups, tiled=True)
 
 
 def side():
     return lax.axis_index("narrow") // (lax.axis_size("narrow") // 2)
 
 
-def pair_sums(total):
-    half = total.shape[0] // 2
-    mine = side()
-    kept = lax.dynamic_slice_in_dim(total, mine * half, half)
-    sent = lax.dynamic_slice_in_dim(total, (1 - mine) * half, half).astype(jnp.bfloat16)
-    taken = partner(sent, "narrow", lax.axis_size("narrow") // 2)
-    return kept + taken.astype(jnp.float32)
+def square_sums(totals):
+    parts = [
+        total.astype(jnp.bfloat16).reshape(4, total.shape[0] // 4, -1) for total in totals
+    ]
+    taken = exchange(jnp.concatenate(parts, axis=1), squares())
+    return jnp.split(jnp.sum(taken.astype(jnp.float32), axis=0), len(totals))
 
 
 def to_chunks(rows):
-    return rows.reshape(lax.axis_size("narrow") // 2, -1, LANES)
+    return rows.astype(jnp.bfloat16).reshape(lax.axis_size("narrow") // 4, -1, LANES)
 
 
-def to_all(chunk):
-    return jnp.broadcast_to(chunk[None], (lax.axis_size("narrow") // 2,) + chunk.shape)
-
-
-def join_pair(mine):
-    other = partner(mine, "narrow", lax.axis_size("narrow") // 2)
-    is_upper = side() == 1
-    lower = jnp.where(is_upper, other, mine)
-    upper = jnp.where(is_upper, mine, other)
-    return jnp.concatenate([lower, upper], axis=1).astype(jnp.float32)
+def to_all(chunk, number):
+    return jnp.broadcast_to(chunk[None], (number,) + chunk.shape)
 
 
 def norm_chunk(chunk, width):
@@ -92,7 +90,6 @@
     cunit = unit_rows(centers).astype(jnp.bfloat16)
     far = partner(cunit[end], "wide", 2**end)
     first, second = unit[:half], unit[half:]
-    parts = []
     for section in range(end):
         at_first, at_second = chosen[section]
         outgoing = jnp.concatenate([jnp.where(at_first, first, second), second])
@@ -101,25 +98,30 @@
         first = jnp.where(at_first, lower, first)
         second = jnp.where(at_second, jnp.where(at_first, upper, lower), second)
         total = local_sums(jnp.concatenate([first, second]), cunit[section])
-        parts.append(to_chunks(pair_sums(total).astype(jnp.bfloat16)))
+        if section == 0:
+            begun = total
+        else:
+            middle = total
     leaving = chosen[end]
     sums = [
-        local_sums(block, jnp.where(leaves, far, cunit[end]))
-        for block, leaves in zip((first, second), leaving)
+        local_sums(block, jnp.where(goes, far, cunit[end]))
+        for block, goes in zip((first, second), leaving)
     ]
-    stays = sum(jnp.where(leaves, 0.0, part) for leaves, part in zip(leaving, sums))
-    leaves = sum(jnp.where(leaves, part, 0.0) for leaves, part in zip(leaving, sums))
-    both = jnp.concatenate([stays.reshape(2, half // 2, width), leaves.reshape(2, half // 2, width)], axis=1)
-    paired = pair_sums(both.reshape(2 * half, width))
-    gone = partner(paired[half // 2 :].astype(jnp.bfloat16), "wide", 2**end)
-    paired = paired[: half // 2] + gone.astype(jnp.float32)
-    parts.append(to_chunks(paired.astype(jnp.bfloat16)))
-    taken = exchange(jnp.concatenate(parts, axis=1))
+    leaves = sum(jnp.where(goes, part, 0.0) for goes, part in zip(leaving, sums))
+    stays = sum(jnp.where(goes, 0.0, part) for goes, part in zip(leaving, sums))
+    leaves, begun, middle, stays = square_sums([leaves, begun, middle, stays])
+    leaves = partner(leaves.astype(jnp.bfloat16), "wide", 2**end)
+    last = stays + leaves.astype(jnp.float32)
+    parts = [to_chunks(part) for part in (begun, middle, last)]
+    taken = exchange(jnp.concatenate(parts, axis=1), rings())
     summed = jnp.sum(taken.astype(jnp.float32), axis=0)
     chunk = norm_chunk(summed, width)
-    taken = exchange(to_all(chunk))
+    taken = exchange(to_all(chunk, taken.shape[0]), rings())
     taken = jnp.moveaxis(taken.reshape(taken.shape[0], sections, -1, LANES), 1, 0)
-    return join_pair(taken.reshape(sections, half // 2, width))
+    taken = taken.reshape(sections, half // 4, width)
+    taken = exchange(to_all(taken, 4), squares())
+    taken = jnp.moveaxis(taken, 0, 1).reshape(sections, half, width)
+    return taken.astype(jnp.float32)
 
 
 def solution(mesh):

time: 138 us -> 125 us (0.906)
  the two profiles are of different devices: /device:TPU:26 before, /device:TPU:8 now
where the time goes in v2:
time: 125 us; the launch traced here: 124 us
  blocking collectives  71.2 us (57%)
  starting transfers between devices  20.8 us (17%)
  waiting for transfers between devices  18.1 us (14%)
  other arithmetic  6.62 us (5%)
  between operations  4.06 us (3%)
  matrix products  2.11 us (2%)
  local copies, waits for them, and re-layouts  1.26 us (1%)
    all_to_all x4, blocking collectives, exchange(): lax.all_to_all(values, 'narrow', 0, 0, axis_index_groups=groups, tiled=True)  71.2 us
    ppermute x4, starting transfers between devices, partner(): return lax.ppermute(value, axis, pairs)  20.8 us
    ppermute x4, waiting for transfers between devices, partner(): return lax.ppermute(value, axis, pairs)  18.1 us
  transfers between devices with their start and end apart: 4, of which 3 were waited for; matrix products, arithmetic and copies ran while one was open for 1% of the time, Pallas kernels for 0%

profile of v2, /device:TPU:8, one launch (start us, length us, event | category | flops | bytes accessed | tf_op | source)
XLA Modules:
  0.0 124.1 jit_solution(9588828294768939667)
XLA Ops:
  0.0 1.2 fusion.6
  1.2 0.8 fusion.28
  2.0 0.7 and_convert_fusion
  2.7 0.7 fusion.27
  3.4 0.0 copy-start
  3.4 1.3 %fusion.7 = bf16[256,1024]{1,0:T(8,128)(2,1)S(1)} fusion(bf16[256,1024]{1,0:T(8,128)(2,1)} %param.4, f32[256]{0:T(256)S(1)} %add_rsqrt_fusion.1), kind=kLoop, calls=%fused_computation.18 | loop fusion | flops 786432 | bytes 1049600 | tf_op jit(solution)/shard_map/convert_element_type | solution.py:89
  5.4 1.9 %collective-permute-start = (bf16[256,1024]{1,0:T(8,128)(2,1)S(1)}, bf16[256,1024]{1,0:T(8,128)(2,1)S(1)}, u32[]{:S(2)}, u32[]{:S(2)}) collective-permute-start(bf16[256,1024]{1,0:T(8,128)(2,1)S(1)} %pad_maximum_fusion.3), channel_id=1, source_target_pairs={{0,32},{32,0},{64,96},{96,64},{128,160},{160,128},{192,224},{224,1... | collective-permute-start | bytes 1572872 | tf_op jit(solution)/shard_map/ppermute | solution.py:13
  7.3 0.0 copy-done
  7.3 0.2 fusion
  8.8 0.2 fusion.1
  9.0 0.2 collective-permute-done
  9.2 0.1 broadcast_select_fusion.3
  9.3 15.0 %collective-permute-start.1 = (bf16[256,1024]{1,0:T(8,128)(2,1)S(1)}, bf16[256,1024]{1,0:T(8,128)(2,1)S(1)}, u32[]{:S(2)}, u32[]{:S(2)}) collective-permute-start(bf16[256,1024]{1,0:T(8,128)(2,1)S(1)} %pad_maximum_fusion.2), channel_id=1, source_target_pairs={{0,64},{32,96},{64,0},{96,32},{128,192},{160,224},{192,128},{224,1... | collective-permute-start | bytes 1572872 | tf_op jit(solution)/shard_map/ppermute | solution.py:13
  24.3 1.9 %collective-permute-start.2 = (bf16[128,1024]{1,0:T(8,128)(2,1)S(1)}, bf16[128,1024]{1,0:T(8,128)(2,1)S(1)}, u32[]{:S(2)}, u32[]{:S(2)}) collective-permute-start(bf16[128,1024]{1,0:T(8,128)(2,1)S(1)} %slice_bitcast_fusion.4), channel_id=1, source_target_pairs={{0,128},{32,160},{64,192},{96,224},{128,0},{160,32},{192,64},{224,... | collective-permute-start | bytes 786440 | tf_op jit(solution)/shard_map/ppermute | solution.py:13
  28.2 0.3 fusion.32
  28.5 0.2 convolution_convert_fusion.1
  28.7 12.9 %collective-permute-done.1 = bf16[256,1024]{1,0:T(8,128)(2,1)S(1)} collective-permute-done((bf16[256,1024]{1,0:T(8,128)(2,1)S(1)}, bf16[256,1024]{1,0:T(8,128)(2,1)S(1)}, u32[]{:S(2)}, u32[]{:S(2)}) %collective-permute-start.1) | collective-permute-done | bytes 524320 | tf_op jit(solution)/shard_map/ppermute | solution.py:13
  41.6 0.1 broadcast_select_fusion.2
  41.7 0.3 fusion.31
  42.0 0.2 convolution_convert_fusion
  42.2 0.0 collective-permute-done.2
  42.2 0.3 fusion.30
  42.5 0.2 fusion.17
  42.7 0.3 fusion.29
  43.0 0.3 add_convert_fusion.1
  43.2 0.1 pad_maximum_fusion
  43.3 16.6 %all_to_all.20 = bf16[4,128,1024]{2,1,0:T(8,128)(2,1)S(1)} all-to-all(bf16[4,128,1024]{2,1,0:T(8,128)(2,1)S(1)} %pad_maximum_fusion), channel_id=1, replica_groups={{0,1,16,17},{2,3,18,19},{4,5,20,21},{6,7,22,23},{8,9,24,25},{10,11,26,2..., dimensions={0} | all-to-all | bytes 2097152 | tf_op jit(solution)/shard_map/all_to_all | solution.py:46
  59.9 0.2 convert_reduce_fusion
  60.1 1.9 %collective-permute-start.3 = (bf16[32,1024]{1,0:T(8,128)(2,1)S(1)}, bf16[32,1024]{1,0:T(8,128)(2,1)S(1)}, u32[]{:S(2)}, u32[]{:S(2)}) collective-permute-start(bf16[32,1024]{1,0:T(8,128)(2,1)S(1)} %get-tuple-element.15), channel_id=1, source_target_pairs={{0,128},{32,160},{64,192},{96,224},{128,0},{160,32},{192,64},{224,... | collective-permute-start | bytes 196616 | tf_op jit(solution)/shard_map/ppermute | solution.py:13
  62.1 5.0 %collective-permute-done.3 = bf16[32,1024]{1,0:T(8,128)(2,1)S(1)} collective-permute-done((bf16[32,1024]{1,0:T(8,128)(2,1)S(1)}, bf16[32,1024]{1,0:T(8,128)(2,1)S(1)}, u32[]{:S(2)}, u32[]{:S(2)}) %collective-permute-start.3) | collective-permute-done | bytes 65568 | tf_op jit(solution)/shard_map/ppermute | solution.py:13
  67.3 24.8 %all_to_all.21 = bf16[8,96,128]{2,1,0:T(8,128)(2,1)S(1)} all-to-all(bf16[8,96,128]{2,1,0:T(8,128)(2,1)S(1)} %pad_maximum_fusion.9), channel_id=1, replica_groups={{0,2,4,6,8,10,12,14},{1,3,5,7,9,11,13,15},{16,18,20,22,24,26,28,30},{17..., dimensions={0} | all-to-all | bytes 393216 | tf_op jit(solution)/shard_map/all_to_all | solution.py:46
  92.1 0.1 multiply_reduce_fusion
  92.2 0.1 reduce_sum.97
  92.3 0.1 reduce_sum.98
  92.5 0.1 mul.66
  92.5 0.1 mul.67
  92.6 0.1 multiply_convert_fusion
  92.8 18.9 %all_to_all.22 = bf16[8,96,128]{2,1,0:T(8,128)(2,1)S(1)} all-to-all(bf16[8,96,128]{2,1,0:T(8,128)(2,1)S(1)} %broadcast_in_dim.15), channel_id=1, replica_groups={{0,2,4,6,8,10,12,14},{1,3,5,7,9,11,13,15},{16,18,20,22,24,26,28,30},{17..., dimensions={0} | all-to-all | bytes 393216 | tf_op jit(solution)/shard_map/all_to_all | solution.py:46
  111.7 0.1 broadcast_in_dim.16
  111.8 0.1 broadcast_in_dim.17
  111.9 10.9 %all_to_all.23 = bf16[4,3,32,1024]{3,2,1,0:T(8,128)(2,1)S(1)} all-to-all(bf16[4,3,32,1024]{3,2,1,0:T(8,128)(2,1)S(1)} %broadcast_in_dim.17), channel_id=1, replica_groups={{0,1,16,17},{2,3,18,19},{4,5,20,21},{6,7,22,23},{8,9,24,25},{10,11,26,2..., dimensions={0} | all-to-all | bytes 1572864 | tf_op jit(solution)/shard_map/all_to_all | solution.py:46
  122.8 1.3 %copy_convert_fusion = f32[4,3,32,1024]{3,2,0,1:T(8,128)} fusion(bf16[4,3,32,1024]{3,2,1,0:T(8,128)(2,1)S(1)} %all_to_all.23), kind=kLoop, calls=%fused_computation.20 | loop fusion | flops 393216 | bytes 2359296 | tf_op jit(solution)/shard_map/convert_element_type | solution.py:124
  (17 shorter events, 0.4 us)
Async XLA Ops:
  3.4 3.9 %copy-start = (bf16[3,128,1024]{2,1,0:T(8,128)(2,1)S(1)}, bf16[3,128,1024]{2,1,0:T(8,128)(2,1)}, u32[]{:S(2)}) copy-start(bf16[3,128,1024]{2,1,0:T(8,128)(2,1)} %param.5) | copy-start | bytes 2359300
  5.4 3.8 %collective-permute-start = (bf16[256,1024]{1,0:T(8,128)(2,1)S(1)}, bf16[256,1024]{1,0:T(8,128)(2,1)S(1)}, u32[]{:S(2)}, u32[]{:S(2)}) collective-permute-start(bf16[256,1024]{1,0:T(8,128)(2,1)S(1)} %pad_maximum_fusion.3), channel_id=1, source_target_pairs={{0,32},{32,0},{64,96},{96,64},{128,160},{160,128},{192,224},{224,1... | collective-permute-start | bytes 1572872 | tf_op jit(solution)/shard_map/ppermute | solution.py:13
  9.3 32.3 %collective-permute-start.1 = (bf16[256,1024]{1,0:T(8,128)(2,1)S(1)}, bf16[256,1024]{1,0:T(8,128)(2,1)S(1)}, u32[]{:S(2)}, u32[]{:S(2)}) collective-permute-start(bf16[256,1024]{1,0:T(8,128)(2,1)S(1)} %pad_maximum_fusion.2), channel_id=1, source_target_pairs={{0,64},{32,96},{64,0},{96,32},{128,192},{160,224},{192,128},{224,1... | collective-permute-start | bytes 1572872 | tf_op jit(solution)/shard_map/ppermute | solution.py:13
  24.3 17.9 %collective-permute-start.2 = (bf16[128,1024]{1,0:T(8,128)(2,1)S(1)}, bf16[128,1024]{1,0:T(8,128)(2,1)S(1)}, u32[]{:S(2)}, u32[]{:S(2)}) collective-permute-start(bf16[128,1024]{1,0:T(8,128)(2,1)S(1)} %slice_bitcast_fusion.4), channel_id=1, source_target_pairs={{0,128},{32,160},{64,192},{96,224},{128,0},{160,32},{192,64},{224,... | collective-permute-start | bytes 786440 | tf_op jit(solution)/shard_map/ppermute | solution.py:13
  60.1 7.1 %collective-permute-start.3 = (bf16[32,1024]{1,0:T(8,128)(2,1)S(1)}, bf16[32,1024]{1,0:T(8,128)(2,1)S(1)}, u32[]{:S(2)}, u32[]{:S(2)}) collective-permute-start(bf16[32,1024]{1,0:T(8,128)(2,1)S(1)} %get-tuple-element.15), channel_id=1, source_target_pairs={{0,128},{32,160},{64,192},{96,224},{128,0},{160,32},{192,64},{224,... | collective-permute-start | bytes 196616 | tf_op jit(solution)/shard_map/ppermute | solution.py:13

commit v3 on v2

--- a/solution.py
+++ b/solution.py
@@ -1,11 +1,14 @@
 import jax
 import jax.numpy as jnp
 from jax import lax
+from jax.experimental import pallas as pl
+from jax.experimental.pallas import tpu as pltpu
 from jax.sharding import PartitionSpec as P
 
 EPS = 1e-06
 SHARPNESS = 80.0
 LANES = 128
+STEP = 32
 
 
 def partner(value, axis, mask):
@@ -72,12 +75,56 @@
     return (rows * lax.rsqrt(mean + EPS)).reshape(chunk.shape).astype(jnp.bfloat16)
 
 
-def chosen_slots(moving, sent_counts):
-    flags, counts = moving.T, sent_counts.T
-    ranks = jnp.concatenate([flags[:1], flags[:1] + flags[1:]]) - 1
-    chosen = ((flags == 1) & (ranks < counts)).astype(jnp.int32)
-    chosen = lax.optimization_barrier(chosen)
-    return [[chosen[slot, section] == 1 for slot in range(2)] for section in range(chosen.shape[1])]
+def enter_kernel(moving, sent_counts, points, centers, unit, outgoing, chosen, cunit):
+    half = points.shape[0] // 2
+    for section in range(moving.shape[1]):
+        rank = -1
+        for slot in range(2):
+            flag = moving[slot, section]
+            rank = rank + flag
+            sends = ((flag == 1) & (rank < sent_counts[0, section])).astype(jnp.int32)
+            row = pl.ds(2 * section + slot, 1)
+            chosen[row] = jnp.full((1, LANES), sends, jnp.int32)
+    at_first = (moving[0, 0] == 1) & (moving[0, 0] - 1 < sent_counts[0, 0])
+    start = pl.multiple_of(jnp.where(at_first, 0, half), STEP)
+
+    @pl.loop(0, points.shape[0] // STEP, unroll=True)
+    def _(at):
+        rows = pl.ds(at * STEP, STEP)
+        unit[rows] = unit_rows(points[rows]).astype(jnp.bfloat16)
+
+    @pl.loop(0, half // STEP, unroll=True)
+    def _(at):
+        outgoing[pl.ds(at * STEP, STEP)] = unit[pl.ds(start + at * STEP, STEP)]
+        rows = pl.ds(half + at * STEP, STEP)
+        outgoing[rows] = unit[rows]
+
+    for section in range(centers.shape[0]):
+
+        @pl.loop(0, centers.shape[1] // STEP, unroll=True)
+        def _(at):
+            rows = pl.ds(at * STEP, STEP)
+            cunit[section, rows] = unit_rows(centers[section, rows]).astype(jnp.bfloat16)
+
+
+def enter(points, centers, moving, sent_counts):
+    return pl.pallas_call(
+        enter_kernel,
+        out_shape=(
+            pltpu.VMEM(points.shape, jnp.bfloat16),
+            pltpu.VMEM(points.shape, jnp.bfloat16),
+            pltpu.VMEM((8, LANES), jnp.int32),
+            pltpu.VMEM(centers.shape, jnp.bfloat16),
+        ),
+        in_specs=[
+            pl.BlockSpec(memory_space=pltpu.SMEM),
+            pl.BlockSpec(memory_space=pltpu.SMEM),
+            pl.BlockSpec(memory_space=pltpu.VMEM),
+            pl.BlockSpec(memory_space=pltpu.VMEM),
+        ],
+        out_specs=(pl.BlockSpec(memory_space=pltpu.VMEM),) * 4,
+        name="enter",
+    )(moving.T, sent_counts.T, points, centers)
 
 
 def on_device(points, centers, moving, sent_counts):
@@ -85,15 +132,17 @@
     sections, _ = moving.shape
     half = rows_dev // 2
     end = sections - 1
-    chosen = chosen_slots(moving, sent_counts)
-    unit = unit_rows(points).astype(jnp.bfloat16)
-    cunit = unit_rows(centers).astype(jnp.bfloat16)
+    unit, sent, flags, cunit = enter(points, centers, moving, sent_counts)
+    chosen = [
+        [flags[2 * section + slot, 0] == 1 for slot in range(2)] for section in range(sections)
+    ]
     far = partner(cunit[end], "wide", 2**end)
     first, second = unit[:half], unit[half:]
     for section in range(end):
         at_first, at_second = chosen[section]
-        outgoing = jnp.concatenate([jnp.where(at_first, first, second), second])
-        incoming = partner(outgoing, "wide", 2**section)
+        if section > 0:
+            sent = jnp.concatenate([jnp.where(at_first, first, second), second])
+        incoming = partner(sent, "wide", 2**section)
         lower, upper = incoming[:half], incoming[half:]
         first = jnp.where(at_first, lower, first)
         second = jnp.where(at_second, jnp.where(at_first, upper, lower), second)

time: 125 us -> 122 us (0.976)
  other arithmetic: 6.62 us -> 2.14 us
  Pallas kernels: 0 us -> 1.77 us
    convert_element_type x3 -> x0, other arithmetic: 2.17 us -> none  [the longest x1 1.27 us: on_device(): unit = unit_rows(points).astype(jnp.bfloat16)]
    pallas_call x0 -> x1, Pallas kernels: none -> 1.77 us  [enter(): pl.pallas_call(enter_kernel, out_shape=(pltpu.VMEM(points.shape, jnp.bflo...]
    reduce_sum x2 -> x0, other arithmetic: 1.46 us -> none  [unit_rows(): jnp.mean(widened * widened, axis=-1, keepdims=True) + EPS]
  transfers between devices with their start and end apart: 4 -> 4, of which waited for: 3 -> 2; matrix products, arithmetic and copies ran while one was open for 1% -> 2% of each run, Pallas kernels for 0% -> 0%
where the time goes in v3:
time: 122 us
  blocking collectives  71.6 us (59%)
  starting transfers between devices  20.8 us (17%)
  waiting for transfers between devices  18.1 us (15%)
  between operations  3.95 us (3%)
  other arithmetic  2.14 us (2%)
  matrix products  2.13 us (2%)
  Pallas kernels  1.77 us (1%)
    all_to_all x4, blocking collectives, exchange(): lax.all_to_all(values, 'narrow', 0, 0, axis_index_groups=groups, tiled=True)  71.6 us
    ppermute x4, starting transfers between devices, partner(): return lax.ppermute(value, axis, pairs)  20.8 us
    ppermute x4, waiting for transfers between devices, partner(): return lax.ppermute(value, axis, pairs)  18.1 us
  transfers between devices with their start and end apart: 4, of which 2 were waited for; matrix products, arithmetic and copies ran while one was open for 2% of the time, Pallas kernels for 0%

profile of v3, /device:TPU:8, one launch (start us, length us, event | category | flops | bytes accessed | tf_op | source)
XLA Modules:
  0.0 121.7 jit_solution(13362303317219103869)
XLA Ops:
  0.0 1.8 %enter.1 = (bf16[256,1024]{1,0:T(8,128)(2,1)S(1)}, bf16[256,1024]{1,0:T(8,128)(2,1)S(1)}, s32[8,128]{1,0:T(8,128)S(1)}, bf16[3,128,1024]{2,1,0:T(8,128)(2,1)S(1)}) custom-call(s32[2,3]{1,0:T(2,128)} %bitcast.51, s32[1,3]{1,0:T(1,128)} %bitcast.52, bf16[256,1024]{1,0:T(8,128)(2,1)} %points.1, bf16[3,128,1024]{2,1,0:T(8,128)(2,1)} %centers.1), custom_call_target="tpu_custom_call" | custom-call | tf_op jit(solution)/shard_map/enter/pallas_call | solution.py:111
  1.8 1.9 %collective-permute-start = (bf16[256,1024]{1,0:T(8,128)(2,1)S(1)}, bf16[256,1024]{1,0:T(8,128)(2,1)S(1)}, u32[]{:S(2)}, u32[]{:S(2)}) collective-permute-start(bf16[256,1024]{1,0:T(8,128)(2,1)S(1)} %get-tuple-element.10), channel_id=1, source_target_pairs={{0,32},{32,0},{64,96},{96,64},{128,160},{160,128},{192,224},{224,1... | collective-permute-start | bytes 1572872 | tf_op jit(solution)/shard_map/ppermute | solution.py:16
  3.7 0.6 fusion.27
  6.2 0.0 collective-permute-done
  6.2 0.1 broadcast_select_fusion.1
  6.3 15.0 %collective-permute-start.1 = (bf16[256,1024]{1,0:T(8,128)(2,1)S(1)}, bf16[256,1024]{1,0:T(8,128)(2,1)S(1)}, u32[]{:S(2)}, u32[]{:S(2)}) collective-permute-start(bf16[256,1024]{1,0:T(8,128)(2,1)S(1)} %pad_maximum_fusion.2), channel_id=1, source_target_pairs={{0,64},{32,96},{64,0},{96,32},{128,192},{160,224},{192,128},{224,1... | collective-permute-start | bytes 1572872 | tf_op jit(solution)/shard_map/ppermute | solution.py:16
  21.3 1.9 %collective-permute-start.2 = (bf16[128,1024]{1,0:T(8,128)(2,1)S(1)}, bf16[128,1024]{1,0:T(8,128)(2,1)S(1)}, u32[]{:S(2)}, u32[]{:S(2)}) collective-permute-start(bf16[128,1024]{1,0:T(8,128)(2,1)S(1)} %slice_bitcast_fusion), channel_id=1, source_target_pairs={{0,128},{32,160},{64,192},{96,224},{128,0},{160,32},{192,64},{224,... | collective-permute-start | bytes 786440 | tf_op jit(solution)/shard_map/ppermute | solution.py:16
  25.1 0.3 fusion.31
  25.4 0.2 convolution_convert_fusion.1
  25.7 13.1 %collective-permute-done.1 = bf16[256,1024]{1,0:T(8,128)(2,1)S(1)} collective-permute-done((bf16[256,1024]{1,0:T(8,128)(2,1)S(1)}, bf16[256,1024]{1,0:T(8,128)(2,1)S(1)}, u32[]{:S(2)}, u32[]{:S(2)}) %collective-permute-start.1) | collective-permute-done | bytes 524320 | tf_op jit(solution)/shard_map/ppermute | solution.py:16
  38.7 0.1 broadcast_select_fusion
  38.8 0.3 fusion.30
  39.1 0.2 convolution_convert_fusion
  39.4 0.0 collective-permute-done.2
  39.4 0.3 fusion.29
  39.7 0.2 fusion.17
  39.9 0.3 fusion.28
  40.1 0.3 add_convert_fusion.1
  40.4 0.1 pad_maximum_fusion
  40.5 16.7 %all_to_all.20 = bf16[4,128,1024]{2,1,0:T(8,128)(2,1)S(1)} all-to-all(bf16[4,128,1024]{2,1,0:T(8,128)(2,1)S(1)} %pad_maximum_fusion), channel_id=1, replica_groups={{0,1,16,17},{2,3,18,19},{4,5,20,21},{6,7,22,23},{8,9,24,25},{10,11,26,2..., dimensions={0} | all-to-all | bytes 2097152 | tf_op jit(solution)/shard_map/all_to_all | solution.py:49
  57.2 0.2 convert_reduce_fusion
  57.5 1.9 %collective-permute-start.3 = (bf16[32,1024]{1,0:T(8,128)(2,1)S(1)}, bf16[32,1024]{1,0:T(8,128)(2,1)S(1)}, u32[]{:S(2)}, u32[]{:S(2)}) collective-permute-start(bf16[32,1024]{1,0:T(8,128)(2,1)S(1)} %get-tuple-element.21), channel_id=1, source_target_pairs={{0,128},{32,160},{64,192},{96,224},{128,0},{160,32},{192,64},{224,... | collective-permute-start | bytes 196616 | tf_op jit(solution)/shard_map/ppermute | solution.py:16
  59.5 5.0 %collective-permute-done.3 = bf16[32,1024]{1,0:T(8,128)(2,1)S(1)} collective-permute-done((bf16[32,1024]{1,0:T(8,128)(2,1)S(1)}, bf16[32,1024]{1,0:T(8,128)(2,1)S(1)}, u32[]{:S(2)}, u32[]{:S(2)}) %collective-permute-start.3) | collective-permute-done | bytes 65568 | tf_op jit(solution)/shard_map/ppermute | solution.py:16
  64.6 25.0 %all_to_all.21 = bf16[8,96,128]{2,1,0:T(8,128)(2,1)S(1)} all-to-all(bf16[8,96,128]{2,1,0:T(8,128)(2,1)S(1)} %pad_maximum_fusion.8), channel_id=1, replica_groups={{0,2,4,6,8,10,12,14},{1,3,5,7,9,11,13,15},{16,18,20,22,24,26,28,30},{17..., dimensions={0} | all-to-all | bytes 393216 | tf_op jit(solution)/shard_map/all_to_all | solution.py:49
  89.6 0.1 multiply_reduce_fusion
  89.7 0.1 reduce_sum.77
  89.8 0.1 reduce_sum.78
  90.0 0.1 mul.38
  90.0 0.1 mul.39
  90.1 0.1 multiply_convert_fusion
  90.3 18.9 %all_to_all.22 = bf16[8,96,128]{2,1,0:T(8,128)(2,1)S(1)} all-to-all(bf16[8,96,128]{2,1,0:T(8,128)(2,1)S(1)} %broadcast_in_dim.15), channel_id=1, replica_groups={{0,2,4,6,8,10,12,14},{1,3,5,7,9,11,13,15},{16,18,20,22,24,26,28,30},{17..., dimensions={0} | all-to-all | bytes 393216 | tf_op jit(solution)/shard_map/all_to_all | solution.py:49
  109.2 0.1 broadcast_in_dim.28
  109.3 0.1 broadcast_in_dim.29
  109.4 10.9 %all_to_all.23 = bf16[4,3,32,1024]{3,2,1,0:T(8,128)(2,1)S(1)} all-to-all(bf16[4,3,32,1024]{3,2,1,0:T(8,128)(2,1)S(1)} %broadcast_in_dim.29), channel_id=1, replica_groups={{0,1,16,17},{2,3,18,19},{4,5,20,21},{6,7,22,23},{8,9,24,25},{10,11,26,2..., dimensions={0} | all-to-all | bytes 1572864 | tf_op jit(solution)/shard_map/all_to_all | solution.py:49
  120.3 1.3 %copy_convert_fusion = f32[4,3,32,1024]{3,2,0,1:T(8,128)} fusion(bf16[4,3,32,1024]{3,2,1,0:T(8,128)(2,1)S(1)} %all_to_all.23), kind=kLoop, calls=%fused_computation.12 | loop fusion | flops 393216 | bytes 2359296 | tf_op jit(solution)/shard_map/convert_element_type | solution.py:173
  (13 shorter events, 0.3 us)
Async XLA Ops:
  1.8 4.4 %collective-permute-start = (bf16[256,1024]{1,0:T(8,128)(2,1)S(1)}, bf16[256,1024]{1,0:T(8,128)(2,1)S(1)}, u32[]{:S(2)}, u32[]{:S(2)}) collective-permute-start(bf16[256,1024]{1,0:T(8,128)(2,1)S(1)} %get-tuple-element.10), channel_id=1, source_target_pairs={{0,32},{32,0},{64,96},{96,64},{128,160},{160,128},{192,224},{224,1... | collective-permute-start | bytes 1572872 | tf_op jit(solution)/shard_map/ppermute | solution.py:16
  6.3 32.5 %collective-permute-start.1 = (bf16[256,1024]{1,0:T(8,128)(2,1)S(1)}, bf16[256,1024]{1,0:T(8,128)(2,1)S(1)}, u32[]{:S(2)}, u32[]{:S(2)}) collective-permute-start(bf16[256,1024]{1,0:T(8,128)(2,1)S(1)} %pad_maximum_fusion.2), channel_id=1, source_target_pairs={{0,64},{32,96},{64,0},{96,32},{128,192},{160,224},{192,128},{224,1... | collective-permute-start | bytes 1572872 | tf_op jit(solution)/shard_map/ppermute | solution.py:16
  21.3 18.1 %collective-permute-start.2 = (bf16[128,1024]{1,0:T(8,128)(2,1)S(1)}, bf16[128,1024]{1,0:T(8,128)(2,1)S(1)}, u32[]{:S(2)}, u32[]{:S(2)}) collective-permute-start(bf16[128,1024]{1,0:T(8,128)(2,1)S(1)} %slice_bitcast_fusion), channel_id=1, source_target_pairs={{0,128},{32,160},{64,192},{96,224},{128,0},{160,32},{192,64},{224,... | collective-permute-start | bytes 786440 | tf_op jit(solution)/shard_map/ppermute | solution.py:16
  57.5 7.1 %collective-permute-start.3 = (bf16[32,1024]{1,0:T(8,128)(2,1)S(1)}, bf16[32,1024]{1,0:T(8,128)(2,1)S(1)}, u32[]{:S(2)}, u32[]{:S(2)}) collective-permute-start(bf16[32,1024]{1,0:T(8,128)(2,1)S(1)} %get-tuple-element.21), channel_id=1, source_target_pairs={{0,128},{32,160},{64,192},{96,224},{128,0},{160,32},{192,64},{224,... | collective-permute-start | bytes 196616 | tf_op jit(solution)/shard_map/ppermute | solution.py:16

commit v4 on v3

--- a/solution.py
+++ b/solution.py
@@ -125,6 +125,20 @@
         out_specs=(pl.BlockSpec(memory_space=pltpu.VMEM),) * 4,
         name="enter",
     )(moving.T, sent_counts.T, points, centers)
+
+
+def hold_kernel(values, _, held):
+    held[...] = values[...]
+
+
+def hold(values, earlier):
+    return pl.pallas_call(
+        hold_kernel,
+        out_shape=pltpu.VMEM(values.shape, values.dtype),
+        in_specs=[pl.BlockSpec(memory_space=pltpu.VMEM)] * 2,
+        out_specs=pl.BlockSpec(memory_space=pltpu.VMEM),
+        name="hold",
+    )(values, earlier)
 
 
 def on_device(points, centers, moving, sent_counts):
@@ -148,17 +162,18 @@
         second = jnp.where(at_second, jnp.where(at_first, upper, lower), second)
         total = local_sums(jnp.concatenate([first, second]), cunit[section])
         if section == 0:
-            begun = total
+            (begun,) = square_sums([total])
         else:
             middle = total
-    leaving = chosen[end]
+    held = hold(flags, begun)
+    leaving = [held[2 * end + slot, 0] == 1 for slot in range(2)]
     sums = [
         local_sums(block, jnp.where(goes, far, cunit[end]))
         for block, goes in zip((first, second), leaving)
     ]
     leaves = sum(jnp.where(goes, part, 0.0) for goes, part in zip(leaving, sums))
     stays = sum(jnp.where(goes, 0.0, part) for goes, part in zip(leaving, sums))
-    leaves, begun, middle, stays = square_sums([leaves, begun, middle, stays])
+    leaves, middle, stays = square_sums([leaves, middle, stays])
     leaves = partner(leaves.astype(jnp.bfloat16), "wide", 2**end)
     last = stays + leaves.astype(jnp.float32)
     parts = [to_chunks(part) for part in (begun, middle, last)]

time: 122 us -> 122 us (level)
  the two profiles are of different devices: /device:TPU:8 before, /device:TPU:4 now
where the time goes in v4:
time: 122 us; the launch traced here: 121 us
  blocking collectives  78.3 us (64%)
  starting transfers between devices  16.7 us (14%)
  waiting for transfers between devices  12.1 us (10%)
  between operations  4.06 us (3%)
  matrix products  2.84 us (2%)
  other arithmetic  2.76 us (2%)
  Pallas kernels  2.68 us (2%)
  local copies, waits for them, and re-layouts  1.78 us (1%)
    all_to_all x4, blocking collectives, exchange(): lax.all_to_all(values, 'narrow', 0, 0, axis_index_groups=groups, tiled=True)  78.3 us
    ppermute x4, starting transfers between devices, partner(): return lax.ppermute(value, axis, pairs)  12.4 us
    ppermute x4, waiting for transfers between devices, partner(): return lax.ppermute(value, axis, pairs)  12.1 us
    all_to_all x1, starting transfers between devices, exchange(): lax.all_to_all(values, 'narrow', 0, 0, axis_index_groups=groups, tiled=True)  4.28 us
  transfers between devices with their start and end apart: 5, of which 3 were waited for; matrix products, arithmetic and copies ran while one was open for 3% of the time, Pallas kernels for 1%

profile of v4, /device:TPU:4, one launch (start us, length us, event | category | flops | bytes accessed | tf_op | source)
XLA Modules:
  0.0 121.2 jit_solution(16419802839017774192)
XLA Ops:
  0.0 1.8 %enter.1 = (bf16[256,1024]{1,0:T(8,128)(2,1)S(1)}, bf16[256,1024]{1,0:T(8,128)(2,1)S(1)}, s32[8,128]{1,0:T(8,128)S(1)}, bf16[3,128,1024]{2,1,0:T(8,128)(2,1)S(1)}) custom-call(s32[2,3]{1,0:T(2,128)} %bitcast.50, s32[1,3]{1,0:T(1,128)} %bitcast.51, bf16[256,1024]{1,0:T(8,128)(2,1)} %points.1, bf16[3,128,1024]{2,1,0:T(8,128)(2,1)} %centers.1), custom_call_target="tpu_custom_call" | custom-call | tf_op jit(solution)/shard_map/enter/pallas_call | solution.py:111
  1.8 0.0 copy-start
  1.8 1.9 %collective-permute-start = (bf16[256,1024]{1,0:T(8,128)(2,1)S(1)}, bf16[256,1024]{1,0:T(8,128)(2,1)S(1)}, u32[]{:S(2)}, u32[]{:S(2)}) collective-permute-start(bf16[256,1024]{1,0:T(8,128)(2,1)S(1)} %get-tuple-element.10), channel_id=1, source_target_pairs={{0,32},{32,0},{64,96},{96,64},{128,160},{160,128},{192,224},{224,1... | collective-permute-start | bytes 1572872 | tf_op jit(solution)/shard_map/ppermute | solution.py:16
  3.7 0.6 fusion.28
  6.2 0.0 collective-permute-done
  6.2 0.1 broadcast_select_fusion.1
  6.3 3.5 %collective-permute-start.1 = (bf16[256,1024]{1,0:T(8,128)(2,1)S(1)}, bf16[256,1024]{1,0:T(8,128)(2,1)S(1)}, u32[]{:S(2)}, u32[]{:S(2)}) collective-permute-start(bf16[256,1024]{1,0:T(8,128)(2,1)S(1)} %pad_maximum_fusion.1), channel_id=1, source_target_pairs={{0,64},{32,96},{64,0},{96,32},{128,192},{160,224},{192,128},{224,1... | collective-permute-start | bytes 1572872 | tf_op jit(solution)/shard_map/ppermute | solution.py:16
  9.8 0.3 fusion.29
  10.2 0.0 copy-done
  10.2 0.9 convolution_convert_fusion.1
  11.1 4.3 %all-to-all-start = ((bf16[4,32,1024]{2,1,0:T(8,128)(2,1)}), bf16[4,32,1024]{2,1,0:T(8,128)(2,1)S(1)}, u32[]{:S(2)}, u32[]{:S(2)}) async-start(bf16[4,32,1024]{2,1,0:T(8,128)(2,1)} %bitcast.5), calls=%async_computation | async-start | bytes 524288 | tf_op jit(solution)/shard_map/all_to_all | solution.py:49
  15.4 4.5 %collective-permute-start.2 = (bf16[128,1024]{1,0:T(8,128)(2,1)S(1)}, bf16[128,1024]{1,0:T(8,128)(2,1)S(1)}, u32[]{:S(2)}, u32[]{:S(2)}) collective-permute-start(bf16[128,1024]{1,0:T(8,128)(2,1)S(1)} %slice_bitcast_fusion), channel_id=1, source_target_pairs={{0,128},{32,160},{64,192},{96,224},{128,0},{160,32},{192,64},{224,... | collective-permute-start | bytes 786440 | tf_op jit(solution)/shard_map/ppermute | solution.py:16
  20.5 6.0 %collective-permute-done.1 = bf16[256,1024]{1,0:T(8,128)(2,1)S(1)} collective-permute-done((bf16[256,1024]{1,0:T(8,128)(2,1)S(1)}, bf16[256,1024]{1,0:T(8,128)(2,1)S(1)}, u32[]{:S(2)}, u32[]{:S(2)}) %collective-permute-start.1) | collective-permute-done | bytes 524320 | tf_op jit(solution)/shard_map/ppermute | solution.py:16
  26.4 0.1 broadcast_select_fusion
  26.5 0.3 fusion.32
  26.8 0.2 convolution_convert_fusion
  27.1 0.0 all-to-all-done
  27.1 0.7 convert_reduce_fusion.1._
  27.8 0.9 hold.1
  28.7 0.6 fusion.27
  30.6 1.4 %collective-permute-done.2 = bf16[128,1024]{1,0:T(8,128)(2,1)S(1)} collective-permute-done((bf16[128,1024]{1,0:T(8,128)(2,1)S(1)}, bf16[128,1024]{1,0:T(8,128)(2,1)S(1)}, u32[]{:S(2)}, u32[]{:S(2)}) %collective-permute-start.2) | collective-permute-done | bytes 262176 | tf_op jit(solution)/shard_map/ppermute | solution.py:16
  32.0 0.3 fusion.31
  32.3 0.2 fusion.17
  32.5 0.3 fusion.30
  32.7 0.3 add_convert_fusion.1
  33.0 0.1 pad_maximum_fusion
  33.1 0.0 copy-start.1
  33.1 14.4 %all_to_all.25 = bf16[4,96,1024]{2,1,0:T(8,128)(2,1)S(1)} all-to-all(bf16[4,96,1024]{2,1,0:T(8,128)(2,1)S(1)} %pad_maximum_fusion), channel_id=1, replica_groups={{0,1,16,17},{2,3,18,19},{4,5,20,21},{6,7,22,23},{8,9,24,25},{10,11,26,2..., dimensions={0} | all-to-all | bytes 1572864 | tf_op jit(solution)/shard_map/all_to_all | solution.py:49
  47.5 0.1 convert_reduce_fusion
  47.7 2.5 %collective-permute-start.3 = (bf16[32,1024]{1,0:T(8,128)(2,1)S(1)}, bf16[32,1024]{1,0:T(8,128)(2,1)S(1)}, u32[]{:S(2)}, u32[]{:S(2)}) collective-permute-start(bf16[32,1024]{1,0:T(8,128)(2,1)S(1)} %get-tuple-element.21), channel_id=1, source_target_pairs={{0,128},{32,160},{64,192},{96,224},{128,0},{160,32},{192,64},{224,... | collective-permute-start | bytes 196616 | tf_op jit(solution)/shard_map/ppermute | solution.py:16
  50.2 0.0 copy-done.1
  50.3 4.7 %collective-permute-done.3 = bf16[32,1024]{1,0:T(8,128)(2,1)S(1)} collective-permute-done((bf16[32,1024]{1,0:T(8,128)(2,1)S(1)}, bf16[32,1024]{1,0:T(8,128)(2,1)S(1)}, u32[]{:S(2)}, u32[]{:S(2)}) %collective-permute-start.3) | collective-permute-done | bytes 65568 | tf_op jit(solution)/shard_map/ppermute | solution.py:16
  55.1 33.1 %all_to_all.26 = bf16[8,96,128]{2,1,0:T(8,128)(2,1)S(1)} all-to-all(bf16[8,96,128]{2,1,0:T(8,128)(2,1)S(1)} %pad_maximum_fusion.8), channel_id=1, replica_groups={{0,2,4,6,8,10,12,14},{1,3,5,7,9,11,13,15},{16,18,20,22,24,26,28,30},{17..., dimensions={0} | all-to-all | bytes 393216 | tf_op jit(solution)/shard_map/all_to_all | solution.py:49
  88.3 0.1 multiply_reduce_fusion
  88.4 0.1 reduce_sum.87
  88.4 0.1 reduce_sum.88
  88.6 0.1 mul.38
  88.7 0.1 mul.39
  88.8 0.1 multiply_convert_fusion
  88.9 19.8 %all_to_all.27 = bf16[8,96,128]{2,1,0:T(8,128)(2,1)S(1)} all-to-all(bf16[8,96,128]{2,1,0:T(8,128)(2,1)S(1)} %broadcast_in_dim.15), channel_id=1, replica_groups={{0,2,4,6,8,10,12,14},{1,3,5,7,9,11,13,15},{16,18,20,22,24,26,28,30},{17..., dimensions={0} | all-to-all | bytes 393216 | tf_op jit(solution)/shard_map/all_to_all | solution.py:49
  108.7 0.1 broadcast_in_dim.28
  108.8 0.1 broadcast_in_dim.29
  108.9 10.9 %all_to_all.28 = bf16[4,3,32,1024]{3,2,1,0:T(8,128)(2,1)S(1)} all-to-all(bf16[4,3,32,1024]{3,2,1,0:T(8,128)(2,1)S(1)} %broadcast_in_dim.29), channel_id=1, replica_groups={{0,1,16,17},{2,3,18,19},{4,5,20,21},{6,7,22,23},{8,9,24,25},{10,11,26,2..., dimensions={0} | all-to-all | bytes 1572864 | tf_op jit(solution)/shard_map/all_to_all | solution.py:49
  119.9 1.3 %copy_convert_fusion = f32[4,3,32,1024]{3,2,0,1:T(8,128)} fusion(bf16[4,3,32,1024]{3,2,1,0:T(8,128)(2,1)S(1)} %all_to_all.28), kind=kLoop, calls=%fused_computation.12 | loop fusion | flops 393216 | bytes 2359296 | tf_op jit(solution)/shard_map/convert_element_type | solution.py:188
  (14 shorter events, 0.3 us)
Async XLA Ops:
  1.8 8.4 %copy-start = (s32[8,128]{1,0:T(8,128)}, s32[8,128]{1,0:T(8,128)S(1)}, u32[]{:S(2)}) copy-start(s32[8,128]{1,0:T(8,128)S(1)} %get-tuple-element.9.values) | copy-start | bytes 12292
  1.8 4.4 %collective-permute-start = (bf16[256,1024]{1,0:T(8,128)(2,1)S(1)}, bf16[256,1024]{1,0:T(8,128)(2,1)S(1)}, u32[]{:S(2)}, u32[]{:S(2)}) collective-permute-start(bf16[256,1024]{1,0:T(8,128)(2,1)S(1)} %get-tuple-element.10), channel_id=1, source_target_pairs={{0,32},{32,0},{64,96},{96,64},{128,160},{160,128},{192,224},{224,1... | collective-permute-start | bytes 1572872 | tf_op jit(solution)/shard_map/ppermute | solution.py:16
  6.3 20.1 %collective-permute-start.1 = (bf16[256,1024]{1,0:T(8,128)(2,1)S(1)}, bf16[256,1024]{1,0:T(8,128)(2,1)S(1)}, u32[]{:S(2)}, u32[]{:S(2)}) collective-permute-start(bf16[256,1024]{1,0:T(8,128)(2,1)S(1)} %pad_maximum_fusion.1), channel_id=1, source_target_pairs={{0,64},{32,96},{64,0},{96,32},{128,192},{160,224},{192,128},{224,1... | collective-permute-start | bytes 1572872 | tf_op jit(solution)/shard_map/ppermute | solution.py:16
  11.1 16.0 %all-to-all-start = ((bf16[4,32,1024]{2,1,0:T(8,128)(2,1)}), bf16[4,32,1024]{2,1,0:T(8,128)(2,1)S(1)}, u32[]{:S(2)}, u32[]{:S(2)}) async-start(bf16[4,32,1024]{2,1,0:T(8,128)(2,1)} %bitcast.5), calls=%async_computation | async-start | bytes 524288 | tf_op jit(solution)/shard_map/all_to_all | solution.py:49
  15.4 16.6 %collective-permute-start.2 = (bf16[128,1024]{1,0:T(8,128)(2,1)S(1)}, bf16[128,1024]{1,0:T(8,128)(2,1)S(1)}, u32[]{:S(2)}, u32[]{:S(2)}) collective-permute-start(bf16[128,1024]{1,0:T(8,128)(2,1)S(1)} %slice_bitcast_fusion), channel_id=1, source_target_pairs={{0,128},{32,160},{64,192},{96,224},{128,0},{160,32},{192,64},{224,... | collective-permute-start | bytes 786440 | tf_op jit(solution)/shard_map/ppermute | solution.py:16
  33.1 17.1 %copy-start.1 = (f32[32,1024]{1,0:T(8,128)S(1)}, f32[32,1024]{1,0:T(8,128)}, u32[]{:S(2)}) copy-start(f32[32,1024]{1,0:T(8,128)} %convert_reduce_fusion.1._) | copy-start | bytes 393220
  47.7 7.3 %collective-permute-start.3 = (bf16[32,1024]{1,0:T(8,128)(2,1)S(1)}, bf16[32,1024]{1,0:T(8,128)(2,1)S(1)}, u32[]{:S(2)}, u32[]{:S(2)}) collective-permute-start(bf16[32,1024]{1,0:T(8,128)(2,1)S(1)} %get-tuple-element.21), channel_id=1, source_target_pairs={{0,128},{32,160},{64,192},{96,224},{128,0},{160,32},{192,64},{224,... | collective-permute-start | bytes 196616 | tf_op jit(solution)/shard_map/ppermute | solution.py:16

commit v5 on v4

--- a/solution.py
+++ b/solution.py
@@ -165,7 +165,7 @@
             (begun,) = square_sums([total])
         else:
             middle = total
-    held = hold(flags, begun)
+    held = hold(flags, begun[:8, :LANES])
     leaving = [held[2 * end + slot, 0] == 1 for slot in range(2)]
     sums = [
         local_sums(block, jnp.where(goes, far, cunit[end]))

time: 122 us -> 124 us (1.016)
  the two profiles are of different devices: /device:TPU:4 before, /device:TPU:60 now
where the time goes in v5:
time: 124 us
  blocking collectives  80.2 us (65%)
  starting transfers between devices  15.5 us (12%)
  waiting for transfers between devices  13.1 us (11%)
  between operations  4.09 us (3%)
  matrix products  3.83 us (3%)
  Pallas kernels  2.46 us (2%)
  local copies, waits for them, and re-layouts  2.33 us (2%)
  other arithmetic  2.11 us (2%)
    all_to_all x4, blocking collectives, exchange(): lax.all_to_all(values, 'narrow', 0, 0, axis_index_groups=groups, tiled=True)  80.2 us
    ppermute x4, waiting for transfers between devices, partner(): return lax.ppermute(value, axis, pairs)  13.1 us
    ppermute x4, starting transfers between devices, partner(): return lax.ppermute(value, axis, pairs)  11.3 us
    all_to_all x1, starting transfers between devices, exchange(): lax.all_to_all(values, 'narrow', 0, 0, axis_index_groups=groups, tiled=True)  4.28 us
  transfers between devices with their start and end apart: 5, of which 3 were waited for; matrix products, arithmetic and copies ran while one was open for 3% of the time, Pallas kernels for 1%

profile of v5, /device:TPU:60, one launch (start us, length us, event | category | flops | bytes accessed | tf_op | source)
XLA Modules:
  0.0 123.6 jit_solution(8688853805052889309)
XLA Ops:
  0.0 1.8 %enter.1 = (bf16[256,1024]{1,0:T(8,128)(2,1)S(1)}, bf16[256,1024]{1,0:T(8,128)(2,1)S(1)}, s32[8,128]{1,0:T(8,128)S(1)}, bf16[3,128,1024]{2,1,0:T(8,128)(2,1)S(1)}) custom-call(s32[2,3]{1,0:T(2,128)} %bitcast.50, s32[1,3]{1,0:T(1,128)} %bitcast.51, bf16[256,1024]{1,0:T(8,128)(2,1)} %points.1, bf16[3,128,1024]{2,1,0:T(8,128)(2,1)} %centers.1), custom_call_target="tpu_custom_call" | custom-call | tf_op jit(solution)/shard_map/enter/pallas_call | solution.py:111
  1.8 0.0 copy-start
  1.8 1.9 %collective-permute-start = (bf16[256,1024]{1,0:T(8,128)(2,1)S(1)}, bf16[256,1024]{1,0:T(8,128)(2,1)S(1)}, u32[]{:S(2)}, u32[]{:S(2)}) collective-permute-start(bf16[256,1024]{1,0:T(8,128)(2,1)S(1)} %get-tuple-element.10), channel_id=1, source_target_pairs={{0,32},{32,0},{64,96},{96,64},{128,160},{160,128},{192,224},{224,1... | collective-permute-start | bytes 1572872 | tf_op jit(solution)/shard_map/ppermute | solution.py:16
  3.7 0.6 fusion.28
  6.2 0.0 collective-permute-done
  6.2 0.1 broadcast_select_fusion.1
  6.3 3.3 %collective-permute-start.1 = (bf16[256,1024]{1,0:T(8,128)(2,1)S(1)}, bf16[256,1024]{1,0:T(8,128)(2,1)S(1)}, u32[]{:S(2)}, u32[]{:S(2)}) collective-permute-start(bf16[256,1024]{1,0:T(8,128)(2,1)S(1)} %pad_maximum_fusion.1), channel_id=1, source_target_pairs={{0,64},{32,96},{64,0},{96,32},{128,192},{160,224},{192,128},{224,1... | collective-permute-start | bytes 1572872 | tf_op jit(solution)/shard_map/ppermute | solution.py:16
  9.6 0.3 fusion.29
  10.0 0.0 copy-done
  10.0 0.9 convolution_convert_fusion.1
  10.9 4.3 %all-to-all-start = ((bf16[4,32,1024]{2,1,0:T(8,128)(2,1)}), bf16[4,32,1024]{2,1,0:T(8,128)(2,1)S(1)}, u32[]{:S(2)}, u32[]{:S(2)}) async-start(bf16[4,32,1024]{2,1,0:T(8,128)(2,1)} %bitcast.5), calls=%async_computation | async-start | bytes 524288 | tf_op jit(solution)/shard_map/all_to_all | solution.py:49
  15.2 4.0 %collective-permute-start.2 = (bf16[128,1024]{1,0:T(8,128)(2,1)S(1)}, bf16[128,1024]{1,0:T(8,128)(2,1)}, u32[]{:S(2)}, u32[]{:S(2)}) collective-permute-start(bf16[128,1024]{1,0:T(8,128)(2,1)S(1)} %slice_bitcast_fusion), channel_id=1, source_target_pairs={{0,128},{32,160},{64,192},{96,224},{128,0},{160,32},{192,64},{224,... | collective-permute-start | bytes 786440 | tf_op jit(solution)/shard_map/ppermute | solution.py:16
  19.9 6.3 %collective-permute-done.1 = bf16[256,1024]{1,0:T(8,128)(2,1)S(1)} collective-permute-done((bf16[256,1024]{1,0:T(8,128)(2,1)S(1)}, bf16[256,1024]{1,0:T(8,128)(2,1)S(1)}, u32[]{:S(2)}, u32[]{:S(2)}) %collective-permute-start.1) | collective-permute-done | bytes 524320 | tf_op jit(solution)/shard_map/ppermute | solution.py:16
  26.2 0.1 broadcast_select_fusion
  26.3 0.3 fusion.32
  26.6 0.2 convolution_convert_fusion
  26.9 0.0 all-to-all-done
  26.9 0.6 slice.68._
  27.5 0.7 hold.1
  28.2 0.5 fusion.27
  30.1 1.9 %collective-permute-done.2 = bf16[128,1024]{1,0:T(8,128)(2,1)} collective-permute-done((bf16[128,1024]{1,0:T(8,128)(2,1)S(1)}, bf16[128,1024]{1,0:T(8,128)(2,1)}, u32[]{:S(2)}, u32[]{:S(2)}) %collective-permute-start.2) | collective-permute-done | bytes 262176 | tf_op jit(solution)/shard_map/ppermute | solution.py:16
  31.9 1.2 fusion.31
  33.1 0.2 fusion.17
  33.4 0.3 fusion.30
  33.6 0.3 add_convert_fusion.1
  33.9 0.1 pad_maximum_fusion
  34.0 15.0 %all_to_all.25 = bf16[4,96,1024]{2,1,0:T(8,128)(2,1)S(1)} all-to-all(bf16[4,96,1024]{2,1,0:T(8,128)(2,1)S(1)} %pad_maximum_fusion), channel_id=1, replica_groups={{0,1,16,17},{2,3,18,19},{4,5,20,21},{6,7,22,23},{8,9,24,25},{10,11,26,2..., dimensions={0} | all-to-all | bytes 1572864 | tf_op jit(solution)/shard_map/all_to_all | solution.py:49
  48.9 0.1 convert_reduce_fusion
  49.1 2.0 %collective-permute-start.3 = (bf16[32,1024]{1,0:T(8,128)(2,1)S(1)}, bf16[32,1024]{1,0:T(8,128)(2,1)S(1)}, u32[]{:S(2)}, u32[]{:S(2)}) collective-permute-start(bf16[32,1024]{1,0:T(8,128)(2,1)S(1)} %get-tuple-element.21), channel_id=1, source_target_pairs={{0,128},{32,160},{64,192},{96,224},{128,0},{160,32},{192,64},{224,... | collective-permute-start | bytes 196616 | tf_op jit(solution)/shard_map/ppermute | solution.py:16
  51.2 4.9 %collective-permute-done.3 = bf16[32,1024]{1,0:T(8,128)(2,1)S(1)} collective-permute-done((bf16[32,1024]{1,0:T(8,128)(2,1)S(1)}, bf16[32,1024]{1,0:T(8,128)(2,1)S(1)}, u32[]{:S(2)}, u32[]{:S(2)}) %collective-permute-start.3) | collective-permute-done | bytes 65568 | tf_op jit(solution)/shard_map/ppermute | solution.py:16
  56.2 34.2 %all_to_all.26 = bf16[8,96,128]{2,1,0:T(8,128)(2,1)S(1)} all-to-all(bf16[8,96,128]{2,1,0:T(8,128)(2,1)S(1)} %pad_maximum_fusion.8), channel_id=1, replica_groups={{0,2,4,6,8,10,12,14},{1,3,5,7,9,11,13,15},{16,18,20,22,24,26,28,30},{17..., dimensions={0} | all-to-all | bytes 393216 | tf_op jit(solution)/shard_map/all_to_all | solution.py:49
  90.5 0.1 multiply_reduce_fusion
  90.6 0.1 reduce_sum.87
  90.6 0.1 reduce_sum.88
  90.8 0.1 mul.38
  90.9 0.1 mul.39
  91.0 0.1 multiply_convert_fusion
  91.1 19.0 %all_to_all.27 = bf16[8,96,128]{2,1,0:T(8,128)(2,1)S(1)} all-to-all(bf16[8,96,128]{2,1,0:T(8,128)(2,1)S(1)} %broadcast_in_dim.15), channel_id=1, replica_groups={{0,2,4,6,8,10,12,14},{1,3,5,7,9,11,13,15},{16,18,20,22,24,26,28,30},{17..., dimensions={0} | all-to-all | bytes 393216 | tf_op jit(solution)/shard_map/all_to_all | solution.py:49
  110.1 0.1 broadcast_in_dim.28
  110.2 0.1 broadcast_in_dim.29
  110.3 12.0 %all_to_all.28 = bf16[4,3,32,1024]{3,2,1,0:T(8,128)(2,1)S(1)} all-to-all(bf16[4,3,32,1024]{3,2,1,0:T(8,128)(2,1)S(1)} %broadcast_in_dim.29), channel_id=1, replica_groups={{0,1,16,17},{2,3,18,19},{4,5,20,21},{6,7,22,23},{8,9,24,25},{10,11,26,2..., dimensions={0} | all-to-all | bytes 1572864 | tf_op jit(solution)/shard_map/all_to_all | solution.py:49
  122.3 1.3 %copy_convert_fusion = f32[4,3,32,1024]{3,2,0,1:T(8,128)} fusion(bf16[4,3,32,1024]{3,2,1,0:T(8,128)(2,1)S(1)} %all_to_all.28), kind=kLoop, calls=%fused_computation.12 | loop fusion | flops 393216 | bytes 2359296 | tf_op jit(solution)/shard_map/convert_element_type | solution.py:188
  (15 shorter events, 0.3 us)
Async XLA Ops:
  1.8 8.2 %copy-start = (s32[8,128]{1,0:T(8,128)}, s32[8,128]{1,0:T(8,128)S(1)}, u32[]{:S(2)}) copy-start(s32[8,128]{1,0:T(8,128)S(1)} %get-tuple-element.9.values) | copy-start | bytes 12292
  1.8 4.4 %collective-permute-start = (bf16[256,1024]{1,0:T(8,128)(2,1)S(1)}, bf16[256,1024]{1,0:T(8,128)(2,1)S(1)}, u32[]{:S(2)}, u32[]{:S(2)}) collective-permute-start(bf16[256,1024]{1,0:T(8,128)(2,1)S(1)} %get-tuple-element.10), channel_id=1, source_target_pairs={{0,32},{32,0},{64,96},{96,64},{128,160},{160,128},{192,224},{224,1... | collective-permute-start | bytes 1572872 | tf_op jit(solution)/shard_map/ppermute | solution.py:16
  6.3 19.9 %collective-permute-start.1 = (bf16[256,1024]{1,0:T(8,128)(2,1)S(1)}, bf16[256,1024]{1,0:T(8,128)(2,1)S(1)}, u32[]{:S(2)}, u32[]{:S(2)}) collective-permute-start(bf16[256,1024]{1,0:T(8,128)(2,1)S(1)} %pad_maximum_fusion.1), channel_id=1, source_target_pairs={{0,64},{32,96},{64,0},{96,32},{128,192},{160,224},{192,128},{224,1... | collective-permute-start | bytes 1572872 | tf_op jit(solution)/shard_map/ppermute | solution.py:16
  10.9 16.0 %all-to-all-start = ((bf16[4,32,1024]{2,1,0:T(8,128)(2,1)}), bf16[4,32,1024]{2,1,0:T(8,128)(2,1)S(1)}, u32[]{:S(2)}, u32[]{:S(2)}) async-start(bf16[4,32,1024]{2,1,0:T(8,128)(2,1)} %bitcast.5), calls=%async_computation | async-start | bytes 524288 | tf_op jit(solution)/shard_map/all_to_all | solution.py:49
  15.2 16.7 %collective-permute-start.2 = (bf16[128,1024]{1,0:T(8,128)(2,1)S(1)}, bf16[128,1024]{1,0:T(8,128)(2,1)}, u32[]{:S(2)}, u32[]{:S(2)}) collective-permute-start(bf16[128,1024]{1,0:T(8,128)(2,1)S(1)} %slice_bitcast_fusion), channel_id=1, source_target_pairs={{0,128},{32,160},{64,192},{96,224},{128,0},{160,32},{192,64},{224,... | collective-permute-start | bytes 786440 | tf_op jit(solution)/shard_map/ppermute | solution.py:16
  49.1 7.1 %collective-permute-start.3 = (bf16[32,1024]{1,0:T(8,128)(2,1)S(1)}, bf16[32,1024]{1,0:T(8,128)(2,1)S(1)}, u32[]{:S(2)}, u32[]{:S(2)}) collective-permute-start(bf16[32,1024]{1,0:T(8,128)(2,1)S(1)} %get-tuple-element.21), channel_id=1, source_target_pairs={{0,128},{32,160},{64,192},{96,224},{128,0},{160,32},{192,64},{224,... | collective-permute-start | bytes 196616 | tf_op jit(solution)/shard_map/ppermute | solution.py:16
